TPU v7x, 32 devices: a whole 2x2x4 slice. The times are simulated.
32 devices in a mesh: expert: 4 (over x, core), hidden: 8 (over z, y).
Axes of the slice: x: 2, y: 2, z: 4, core: 2. Of those that a mesh axis runs over, the one named last changes fastest.
Arguments:
- tokens: bfloat16 [64, 6144], P(('expert', 'hidden')), may hold values from -6 to 6
- routing: int32 [64, 2], P(('expert', 'hidden')), may hold values from 0 to 3, all different within a row; in each aligned block of 2 rows (0 to 1, 2 to 3, ...) at most 2 rows name the same one
- mix_weights: float32 [64, 2], P(('expert', 'hidden')), may hold values from 0.2 to 1
- gate_weight: bfloat16 [4, 6144, 16384], P('expert', None, 'hidden'), may hold values from -0.078125 to 0.078125
- up_weight: bfloat16 [4, 6144, 16384], P('expert', None, 'hidden'), may hold values from -0.078125 to 0.078125
- down_weight: bfloat16 [4, 16384, 6144], P('expert', 'hidden'), may hold values from -0.0625 to 0.0625
Outputs:
- mixed: bfloat16 [64, 6144], P(('expert', 'hidden'))
Inputs may be any that keep to these rules, and one draw needn't show every extreme that they name: `routing`: each row names two different experts. Within each aligned block of 2 rows (the tokens of one device) no expert is named by more than 2 entries, and in every draw some expert is named by exactly 2 entries of some block.
All inputs are finite; a program needn't handle non-finite values.
Results may differ from a plain program's by a relative error of at most 0.0058.
Values may be sent and summed in bfloat16 or wider, within the bound.
A program may use at most 128 MiB of HBM per device.

v0:
```python
import jax
import jax.numpy as jnp
from jax import lax
from jax.sharding import PartitionSpec as P

CAP = 2


def shards(tokens, routing, mix_weights, gate_weight, up_weight, down_weight):
    tok_rows = tokens.shape[0]
    model_width = tokens.shape[1]
    n_expert = lax.axis_size("expert")
    n_hidden = lax.axis_size("hidden")
    entries = routing.reshape(-1)
    one_hot = (entries[:, None] == jnp.arange(n_expert, dtype=jnp.int32)[None, :]).astype(jnp.int32)
    positions = jnp.arange(2 * tok_rows, dtype=jnp.int32)
    before = (positions[None, :] < positions[:, None]).astype(jnp.int32)
    earlier = jnp.sum(before[:, :, None] * one_hot[None, :, :], axis=1)
    slot_ids = jnp.sum(earlier * one_hot, axis=1)
    places = entries * CAP + slot_ids
    send_rows = n_expert * CAP
    row_ids = jnp.arange(send_rows, dtype=jnp.int32)
    place_pairs = places.reshape(tok_rows, 2)
    select = jnp.any(row_ids[:, None, None] == place_pairs[None, :, :], axis=2).astype(jnp.bfloat16)
    outgoing = jnp.dot(select, tokens, preferred_element_type=jnp.float32).astype(jnp.bfloat16)
    arrived = lax.all_to_all(outgoing, "expert", split_axis=0, concat_axis=0, tiled=True)
    w_gate = gate_weight[0]
    w_up = up_weight[0]
    w_down = down_weight[0]
    block_rows = lax.all_gather(arrived, "hidden", axis=0, tiled=True)
    gate_out = jnp.dot(block_rows, w_gate, preferred_element_type=jnp.float32)
    up_out = jnp.dot(block_rows, w_up, preferred_element_type=jnp.float32)
    hidden = (jax.nn.silu(gate_out) * up_out).astype(jnp.bfloat16)
    terms = jnp.dot(hidden, w_down, preferred_element_type=jnp.float32)
    by_row = terms.reshape(n_hidden, send_rows, model_width)
    received = lax.all_to_all(by_row, "hidden", split_axis=0, concat_axis=0, tiled=True)
    finished = jnp.sum(received, axis=0).astype(jnp.bfloat16)
    returned = lax.all_to_all(finished, "expert", split_axis=0, concat_axis=0, tiled=True)
    chooser = (places[:, None] == row_ids[None, :]).astype(jnp.bfloat16)
    picked = jnp.dot(chooser, returned, preferred_element_type=jnp.float32).reshape(
        tok_rows, 2, model_width
    )
    return jnp.sum(mix_weights[:, :, None] * picked, axis=1).astype(jnp.bfloat16)


def solution(mesh):
    in_specs = (
        P(("expert", "hidden"), None),
        P(("expert", "hidden"), None),
        P(("expert", "hidden"), None),
        P("expert", None, "hidden"),
        P("expert", None, "hidden"),
        P("expert", "hidden", None),
    )
    out_specs = P(("expert", "hidden"), None)
    return jax.shard_map(shards, mesh=mesh, in_specs=in_specs, out_specs=out_specs, check_vma=False)
```

profile of v0, /device:TPU:0, one launch (start us, length us, event | category | flops | bytes accessed | tf_op | source)
XLA Modules:
  0.0 118.0 jit_solution(9644648362954346296)
XLA Ops:
  0.0 0.0 copy-start
  0.0 0.8 eq.59
  0.8 0.1 fusion.27
  0.8 0.1 multiply_reduce_fusion
  0.9 0.2 select_reduce_fusion
  1.1 0.1 reduce_sum.40
  1.2 0.7 multiply_add_fusion
  1.9 0.1 compare_reduce_fusion
  2.0 0.0 copy-done
  2.0 0.2 convolution_convert_fusion
  2.2 0.1 all_to_all.17
  2.3 8.3 %all_to_all.26 = bf16[4,2,6144]{2,1,0:T(2,128)(2,1)S(1)} all-to-all(bf16[4,2,6144]{2,1,0:T(2,128)(2,1)S(1)} %all_to_all.17), channel_id=1, replica_groups=mesh['expert'=4,'hidden'=8] {'expert'}, dimensions={0} | all-to-all | bytes 196608 | tf_op jit(solution)/shard_map/all_to_all | solution.py:26
  10.6 32.4 %all_gather.3 = bf16[64,6144]{1,0:T(8,128)(2,1)S(1)} all-gather(bf16[8,6144]{1,0:T(8,128)(2,1)S(1)} %all_to_all.19), channel_id=1, replica_groups=mesh['expert'=4,'hidden'=8] {'hidden'}, dimensions={0}, use_global_device_ids=true | all-gather | bytes 884736 | tf_op jit(solution)/shard_map/all_gather | solution.py:30
  43.0 10.5 %fusion.4 = f32[64,2048]{1,0:T(8,128)S(1)} fusion(bf16[64,6144]{1,0:T(8,128)(2,1)S(1)} %all_gather.3, bf16[1,6144,2048]{2,1,0:T(8,128)(2,1)} %param.9), kind=kOutput, calls=%fused_computation.4 | convolution fusion | flops 1610612736 | bytes 26476544 | tf_op jit(solution)/shard_map/dot_general | solution.py:31
  53.6 0.0 copy-start.1
  53.6 20.0 %fusion = f32[8,8,6144]{2,1,0:T(8,128)S(1)} fusion(bf16[1,2048,6144]{2,1,0:T(8,128)(2,1)} %param.11, bf16[64,6144]{1,0:T(8,128)(2,1)S(1)} %all_gather.3, bf16[1,6144,2048]{2,1,0:T(8,128)(2,1)} %param.10, f32[64,2048]{1,0:T(8,128)S(1)} %fusion.4), kind=kOutput, calls=%fused_computation | convolution fusion | flops 3222011904 | bytes 53215232 | tf_op jit(solution)/shard_map/dot_general | solution.py:34
  73.5 36.6 %all_to_all.27 = f32[8,8,6144]{2,1,0:T(8,128)S(1)} all-to-all(f32[8,8,6144]{2,1,0:T(8,128)S(1)} %fusion), channel_id=1, replica_groups=mesh['expert'=4,'hidden'=8] {'hidden'}, dimensions={0} | all-to-all | bytes 3145728 | tf_op jit(solution)/shard_map/all_to_all | solution.py:36
  110.1 0.1 reduce_sum.41
  110.2 0.1 convert_element_type.37
  110.3 6.7 %all_to_all.28 = bf16[4,2,6144]{2,1,0:T(2,128)(2,1)S(1)} all-to-all(bf16[4,2,6144]{2,1,0:T(2,128)(2,1)S(1)} %convert_element_type.37), channel_id=1, replica_groups=mesh['expert'=4,'hidden'=8] {'expert'}, dimensions={0} | all-to-all | bytes 196608 | tf_op jit(solution)/shard_map/all_to_all | solution.py:38
  117.0 0.0 copy-done.1
  117.0 1.0 fusion.17
  (2 shorter events, 0.1 us)
Async XLA Ops:
  0.0 2.0 %copy-start = (bf16[2,6144]{1,0:T(2,128)(2,1)S(1)}, bf16[2,6144]{1,0:T(2,128)(2,1)}, u32[]{:S(2)}) copy-start(bf16[2,6144]{1,0:T(2,128)(2,1)} %param.6) | copy-start | bytes 73732
  53.6 63.5 %copy-start.1 = (f32[2,2]{1,0:T(2,128)S(1)}, f32[2,2]{1,0:T(2,128)}, u32[]{:S(2)}) copy-start(f32[2,2]{1,0:T(2,128)} %param.8) | copy-start | bytes 52
where the time goes:
time: 118 us
  blocking collectives  84 us (71%)
  matrix products  31.7 us (27%)
  other arithmetic  1.2 us (1%)
    all_to_all x1, blocking collectives, shards(): lax.all_to_all(by_row, 'hidden', split_axis=0, concat_axis=0, tiled=True)  36.6 us
    all_gather x1, blocking collectives, shards(): block_rows = lax.all_gather(arrived, 'hidden', axis=0, tiled=True)  32.4 us
    dot_general x1, matrix products, shards(): terms = jnp.dot(hidden, w_down, preferred_element_type=jnp.float32)  20 us
    dot_general x1, matrix products, shards(): gate_out = jnp.dot(block_rows, w_gate, preferred_element_type=jnp.float32)  10.5 us
    all_to_all x1, blocking collectives, shards(): lax.all_to_all(outgoing, 'expert', split_axis=0, concat_axis=0, tiled=True)  8.31 us
    all_to_all x1, blocking collectives, shards(): lax.all_to_all(finished, 'expert', split_axis=0, concat_axis=0, tiled=True)  6.67 us

commit v1 on v0

v1 whole, which is shorter than its diff:
```python
import functools

import jax
import jax.numpy as jnp
from jax import lax
from jax.experimental import pallas as pl
from jax.experimental.pallas import tpu as pltpu
from jax.sharding import PartitionSpec as P

MESH = pl.DeviceIdType.MESH
LANES = 128
F32 = jnp.float32
BF16 = jnp.bfloat16


def flip(index, stride):
    return index + stride - 2 * stride * lax.rem(lax.div(index, stride), 2)


def kernel(
    cfg, tok_ref, routing_ref, mix_ref, gate_ref, up_ref, down_ref, out_ref,
    w_gate, w_up, w_down, blk, st1, rl, xg, hid, terms, got1, acc, send2, got2, rl2, send3, got3,
    sem_tok, sem_gate, sem_up, sem_down,
    d1_s, d1_r, d2_s, d2_r, d3_s, d3_r, c1_s, c1_r, c2_s, c2_r, c3_s, c3_r,
):
    n_exp, n_hid, T, parts, Nc, FC, nF, NS, J, Ncol, ahead = cfg
    rows = n_hid * T
    e = lax.axis_index("expert")
    h = lax.axis_index("hidden")
    core = flip(e, 1)
    side = flip(e, 2)

    def gate_copy(i, slot):
        return pltpu.make_async_copy(
            gate_ref.at[0, :, pl.ds(pl.multiple_of(i * FC, FC), FC)], w_gate.at[slot], sem_gate.at[slot])

    def up_copy(i, slot):
        return pltpu.make_async_copy(
            up_ref.at[0, :, pl.ds(pl.multiple_of(i * FC, FC), FC)], w_up.at[slot], sem_up.at[slot])

    def down_copy(j):
        return pltpu.make_async_copy(
            down_ref.at[0, :, pl.ds(pl.multiple_of(j * Ncol, Ncol), Ncol)], w_down.at[j], sem_down.at[j])

    def tok_copy(c):
        return pltpu.make_async_copy(
            tok_ref.at[:, pl.ds(c * Nc, Nc)], blk.at[c, :, pl.ds(0, Nc)], sem_tok.at[c])

    for c in range(parts):
        tok_copy(c).start()
    for i in range(NS):
        gate_copy(i, i).start()
        up_copy(i, i).start()
    for j in range(ahead):
        down_copy(j).start()

    barrier = pltpu.get_barrier_semaphore()

    def greet(k, carry):
        pl.semaphore_signal(barrier, inc=1, device_id=(e, lax.rem(h + k, n_hid)), device_id_type=MESH)
        return carry

    lax.fori_loop(1, n_hid, greet, 0)
    pl.semaphore_signal(barrier, inc=1, device_id=(core, h), device_id_type=MESH)
    pl.semaphore_signal(barrier, inc=1, device_id=(side, h), device_id_type=MESH)

    lane = lax.broadcasted_iota(jnp.int32, (T, LANES), 1)
    named = lax.rem(lane, n_exp)
    weight = jnp.zeros((T, LANES), F32)
    for k in range(2):
        weight = weight + jnp.where(named == routing_ref[:, k:k + 1], mix_ref[:, k:k + 1], 0.0)
    high = weight.astype(BF16).astype(F32)
    middle = (weight - high).astype(BF16).astype(F32)
    low = weight - high - middle
    meta = jnp.where(lane < n_exp, high,
                     jnp.where(lane < 2 * n_exp, middle, jnp.where(lane < 3 * n_exp, low, 0.0))).astype(BF16)
    for c in range(parts):
        blk[c, :, Nc:] = meta
        tok_copy(c).wait()

    pl.semaphore_wait(barrier, n_hid + 1)

    def spread(c, k):
        to = lax.rem(h + k, n_hid)
        return pltpu.make_async_remote_copy(
            src_ref=blk.at[c], dst_ref=st1.at[c, h], send_sem=d1_s.at[c, to], recv_sem=d1_r.at[c, h],
            device_id=(e, to), device_id_type=MESH)

    def spread_in(c, k):
        src = lax.rem(h + k, n_hid)
        return pltpu.make_async_remote_copy(
            src_ref=blk.at[c], dst_ref=st1.at[c, src], send_sem=d1_s.at[c, src], recv_sem=d1_r.at[c, src],
            device_id=(e, src), device_id_type=MESH)

    def to_side(c):
        return pltpu.make_async_remote_copy(
            src_ref=xg.at[c, e], dst_ref=xg.at[c, e], send_sem=d2_s.at[c], recv_sem=d2_r.at[c],
            device_id=(side, h), device_id_type=MESH)

    def from_side(c):
        return pltpu.make_async_remote_copy(
            src_ref=xg.at[c, e], dst_ref=xg.at[c, side], send_sem=d2_s.at[c], recv_sem=d2_r.at[c],
            device_id=(side, h), device_id_type=MESH)

    def to_core(c, m):
        group = side if m else e
        return pltpu.make_async_remote_copy(
            src_ref=xg.at[c, group], dst_ref=xg.at[c, group], send_sem=d3_s.at[c, m], recv_sem=d3_r.at[c, m],
            device_id=(core, h), device_id_type=MESH)

    def from_core(c, m):
        group = flip(core, 2) if m else core
        return pltpu.make_async_remote_copy(
            src_ref=xg.at[c, e], dst_ref=xg.at[c, group], send_sem=d3_s.at[c, m], recv_sem=d3_r.at[c, m],
            device_id=(core, h), device_id_type=MESH)

    for c in range(parts):
        def body(k, carry, c=c):
            spread(c, k).start()
            return carry
        lax.fori_loop(1, n_hid, body, 0)
        st1[c, h] = blk[c]
    for c in range(parts):
        def body(k, carry, c=c):
            spread_in(c, k).wait_recv()
            return carry
        lax.fori_loop(1, n_hid, body, 0)
        for k in range(n_hid):
            rl[k * T:(k + 1) * T, :] = st1[c, k].astype(F32)
        xg[c, e] = rl[...].astype(BF16)
        to_side(c).start()
        to_core(c, 0).start()
    for c in range(parts):
        from_side(c).wait_recv()
        to_core(c, 1).start()
    for c in range(parts):
        from_core(c, 0).wait_recv()
        from_core(c, 1).wait_recv()

    def ffn(i, carry):
        slot = lax.rem(i, NS)
        gate_copy(i, slot).wait()
        up_copy(i, slot).wait()
        g = jnp.zeros((n_exp * rows, FC), F32)
        u = jnp.zeros((n_exp * rows, FC), F32)
        for c in range(parts):
            x = xg[c, :, :, 0:Nc].reshape(n_exp * rows, Nc)
            g = g + jnp.dot(x, w_gate[slot, c * Nc:(c + 1) * Nc, :], preferred_element_type=F32)
            u = u + jnp.dot(x, w_up[slot, c * Nc:(c + 1) * Nc, :], preferred_element_type=F32)
        hid[i] = (g / (1.0 + jnp.exp(-g)) * u).astype(BF16)

        @pl.when(i + NS < nF)
        def _():
            gate_copy(i + NS, slot).start()
            up_copy(i + NS, slot).start()

        @pl.when(i == max(nF - NS - 1, 0))
        def _():
            for j in range(ahead, J):
                down_copy(j).start()
        return carry

    lax.fori_loop(0, nF, ffn, 0)

    meta_all = xg[0, :, :, Nc:].reshape(n_exp * rows, LANES).astype(F32)
    lanes = lax.broadcasted_iota(jnp.int32, (n_exp * rows, LANES), 1)
    scale = jnp.sum(jnp.where(lax.rem(lanes, n_exp) == e, meta_all, 0.0), axis=1, keepdims=True)

    def give_core(j, m):
        group = flip(core, 2) if m else core
        return pltpu.make_async_remote_copy(
            src_ref=terms.at[j, group], dst_ref=got1.at[j, m], send_sem=c1_s.at[j, m], recv_sem=c1_r.at[j, m],
            device_id=(core, h), device_id_type=MESH)

    def give_side(j):
        return pltpu.make_async_remote_copy(
            src_ref=send2.at[j], dst_ref=got2.at[j], send_sem=c2_s.at[j], recv_sem=c2_r.at[j],
            device_id=(side, h), device_id_type=MESH)

    def give(j, k):
        to = lax.rem(h + k, n_hid)
        return pltpu.make_async_remote_copy(
            src_ref=send3.at[j, to], dst_ref=got3.at[j, h], send_sem=c3_s.at[j, to], recv_sem=c3_r.at[j, h],
            device_id=(e, to), device_id_type=MESH)

    def take(j, k):
        src = lax.rem(h + k, n_hid)
        return pltpu.make_async_remote_copy(
            src_ref=send3.at[j, src], dst_ref=got3.at[j, src], send_sem=c3_s.at[j, src], recv_sem=c3_r.at[j, src],
            device_id=(e, src), device_id_type=MESH)

    def step(i, carry):
        @pl.when(i < J)
        def _():
            down_copy(i).wait()
            t = jnp.zeros((n_exp * rows, Ncol), F32)
            for k in range(nF):
                t = t + jnp.dot(hid[k], w_down[i, k * FC:(k + 1) * FC, :], preferred_element_type=F32)
            terms[i] = (t * scale).reshape(n_exp, rows, Ncol)
            give_core(i, 1).start()
            give_core(i, 0).start()

        @pl.when(jnp.logical_and(i >= 1, i < J + 1))
        def _():
            j = i - 1
            give_core(j, 1).wait_recv()
            send2[j] = (terms[j, side] + got1[j, 1]).astype(BF16)
            give_side(j).start()
            give_core(j, 0).wait_recv()
            acc[j] = terms[j, e] + got1[j, 0]

        @pl.when(i >= 2)
        def _():
            j = i - 2
            give_side(j).wait_recv()
            rl2[...] = acc[j] + got2[j].astype(F32)
            for k in range(n_hid):
                send3[j, k] = rl2[k * T:(k + 1) * T, :].astype(BF16)

            def body(k, c):
                give(j, k).start()
                return c
            lax.fori_loop(1, n_hid, body, 0)
            got3[j, h] = send3[j, h]
        return carry

    lax.fori_loop(0, J + 2, step, 0)

    for j in range(J):
        def body(k, carry, j=j):
            take(j, k).wait_recv()
            return carry
        lax.fori_loop(1, n_hid, body, 0)
        out_ref[:, j * Ncol:(j + 1) * Ncol] = jnp.sum(got3[j].astype(F32), axis=0).astype(BF16)

    for c in range(parts):
        def body(k, carry, c=c):
            spread(c, k).wait_send()
            return carry
        lax.fori_loop(1, n_hid, body, 0)
        to_side(c).wait_send()
        to_core(c, 0).wait_send()
        to_core(c, 1).wait_send()

    def sent(j, carry):
        give_core(j, 0).wait_send()
        give_core(j, 1).wait_send()
        give_side(j).wait_send()

        def body(k, c):
            give(j, k).wait_send()
            return c
        return lax.fori_loop(1, n_hid, body, carry)
    lax.fori_loop(0, J, sent, 0)


def shards(tokens, routing, mix_weights, gate_weight, up_weight, down_weight):
    T, D = tokens.shape
    FFl = gate_weight.shape[2]
    n_exp = lax.axis_size("expert")
    n_hid = lax.axis_size("hidden")
    assert n_exp == 4
    parts = 2
    Nc = D // parts
    FC = min(256, FFl)
    nF = FFl // FC
    NS = min(5, nF)
    J = 8
    Ncol = D // J
    ahead = min(3, J)
    rows = n_hid * T
    Nw = Nc + LANES
    cfg = (n_exp, n_hid, T, parts, Nc, FC, nF, NS, J, Ncol, ahead)
    dma = pltpu.SemaphoreType.DMA
    scratch = [
        pltpu.VMEM((NS, D, FC), BF16),
        pltpu.VMEM((NS, D, FC), BF16),
        pltpu.VMEM((J, FFl, Ncol), BF16),
        pltpu.VMEM((parts, T, Nw), BF16),
        pltpu.VMEM((parts, n_hid, T, Nw), BF16),
        pltpu.VMEM((rows, Nw), F32),
        pltpu.VMEM((parts, n_exp, rows, Nw), BF16),
        pltpu.VMEM((nF, n_exp * rows, FC), BF16),
        pltpu.VMEM((J, n_exp, rows, Ncol), F32),
        pltpu.VMEM((J, 2, rows, Ncol), F32),
        pltpu.VMEM((J, rows, Ncol), F32),
        pltpu.VMEM((J, rows, Ncol), BF16),
        pltpu.VMEM((J, rows, Ncol), BF16),
        pltpu.VMEM((rows, Ncol), F32),
        pltpu.VMEM((J, n_hid, T, Ncol), BF16),
        pltpu.VMEM((J, n_hid, T, Ncol), BF16),
        dma((parts,)), dma((NS,)), dma((NS,)), dma((J,)),
        dma((parts, n_hid)), dma((parts, n_hid)),
        dma((parts,)), dma((parts,)),
        dma((parts, 2)), dma((parts, 2)),
        dma((J, 2)), dma((J, 2)),
        dma((J,)), dma((J,)),
        dma((J, n_hid)), dma((J, n_hid)),
    ]
    any_spec = pl.BlockSpec(memory_space=pl.ANY)
    vmem = pl.BlockSpec(memory_space=pltpu.VMEM)
    flops = 6 * n_exp * rows * D * FFl
    return pl.pallas_call(
        functools.partial(kernel, cfg),
        out_shape=jax.ShapeDtypeStruct((T, D), BF16),
        in_specs=[any_spec, vmem, vmem, any_spec, any_spec, any_spec],
        out_specs=vmem,
        scratch_shapes=scratch,
        cost_estimate=pl.CostEstimate(flops=flops, bytes_accessed=6 * D * FFl, transcendentals=0),
        compiler_params=pltpu.CompilerParams(
            collective_id=0, has_side_effects=True, vmem_limit_bytes=63 * 1024 * 1024),
    )(tokens, routing, mix_weights, gate_weight, up_weight, down_weight)


def solution(mesh):
    in_specs = (
        P(("expert", "hidden"), None),
        P(("expert", "hidden"), None),
        P(("expert", "hidden"), None),
        P("expert", None, "hidden"),
        P("expert", None, "hidden"),
        P("expert", "hidden", None),
    )
    out_specs = P(("expert", "hidden"), None)
    return jax.shard_map(shards, mesh=mesh, in_specs=in_specs, out_specs=out_specs, check_vma=False)
```

time: 118 us -> 65 us (0.55)
  blocking collectives: 84 us -> 0 us
  Pallas kernels: 0 us -> 63.4 us
  matrix products: 31.7 us -> 0 us
  other arithmetic: 1.2 us -> 0 us
    pallas_call x0 -> x1, Pallas kernels: none -> 63.4 us  [shards(): pl.pallas_call(functools.partial(kernel, cfg), out_shape=jax.ShapeDtypeSt...]
    all_to_all x3 -> x0, blocking collectives: 51.6 us -> none  [the longest x1 36.6 us: shards(): lax.all_to_all(by_row, 'hidden', split_axis=0, concat_axis=0, tiled=True)]
    all_gather x1 -> x0, blocking collectives: 32.4 us -> none  [shards(): block_rows = lax.all_gather(arrived, 'hidden', axis=0, tiled=True)]
    dot_general x4 -> x0, matrix products: 31.7 us -> none  [the longest x1 20 us: shards(): terms = jnp.dot(hidden, w_down, preferred_element_type=jnp.float32)]
    unnamed x4 -> x1, local copies, waits for them, and re-layouts: 0.01 us -> 1.36 us
where the time goes in v1:
time: 65 us; the launch traced here: 64.8 us
  Pallas kernels  63.4 us (98%)
  local copies, waits for them, and re-layouts  1.36 us (2%)
    pallas_call x1, Pallas kernels, shards(): pl.pallas_call(functools.partial(kernel, cfg), out_shape=jax.ShapeDtypeSt...  63.4 us
    unnamed x1, local copies, waits for them, and re-layouts  1.36 us

profile of v1, /device:TPU:0, one launch (start us, length us, event | category | flops | bytes accessed | tf_op | source)
XLA Modules:
  0.0 64.8 jit_solution(10983197433198884742)
XLA Ops:
  0.0 63.4 %shard_map.64 = bf16[2,6144]{1,0:T(2,128)(2,1)} custom-call(bf16[2,6144]{1,0:T(2,128)(2,1)} %tok_ref.1, s32[2,2]{1,0:T(2,128)} %routing_ref.1, f32[2,2]{1,0:T(2,128)} %mix_ref.1, bf16[1,6144,2048]{2,1,0:T(8,128)(2,1)} %gate_ref.1, bf16[1,6144,2048]{2,1,0:T(8,128)(2,1)} %up_ref.1, bf16[1,2048,6144]{2,1,0:T(8,128)(2,1)} %down_ref.1), custom_call_target="tpu_custom_call" | custom-call | flops 4831838208 | bytes 75497472 | tf_op jit(solution)/shard_map/pallas_call | solution.py:303
  63.4 1.4 %copy.8 = bf16[2,6144]{1,0:T(2,128)(2,1)} copy(bf16[2,6144]{1,0:T(2,128)(2,1)} %shard_map.64) | data formatting | bytes 49152

commit v2 on v1

--- a/solution.py
+++ b/solution.py
@@ -19,7 +19,7 @@
 
 def kernel(
     cfg, tok_ref, routing_ref, mix_ref, gate_ref, up_ref, down_ref, out_ref,
-    w_gate, w_up, w_down, blk, st1, rl, xg, hid, terms, got1, acc, send2, got2, rl2, send3, got3,
+    w_gu, w_down, blk, st1, rl, xg, xs, part_sum, hid, terms, got1, acc, send2, got2, rl2, send3, got3,
     sem_tok, sem_gate, sem_up, sem_down,
     d1_s, d1_r, d2_s, d2_r, d3_s, d3_r, c1_s, c1_r, c2_s, c2_r, c3_s, c3_r,
 ):
@@ -32,11 +32,11 @@
 
     def gate_copy(i, slot):
         return pltpu.make_async_copy(
-            gate_ref.at[0, :, pl.ds(pl.multiple_of(i * FC, FC), FC)], w_gate.at[slot], sem_gate.at[slot])
+            gate_ref.at[0, :, pl.ds(pl.multiple_of(i * FC, FC), FC)], w_gu.at[slot, :, pl.ds(0, FC)], sem_gate.at[slot])
 
     def up_copy(i, slot):
         return pltpu.make_async_copy(
-            up_ref.at[0, :, pl.ds(pl.multiple_of(i * FC, FC), FC)], w_up.at[slot], sem_up.at[slot])
+            up_ref.at[0, :, pl.ds(pl.multiple_of(i * FC, FC), FC)], w_gu.at[slot, :, pl.ds(FC, FC)], sem_up.at[slot])
 
     def down_copy(j):
         return pltpu.make_async_copy(
@@ -83,14 +83,12 @@
     def spread(c, k):
         to = lax.rem(h + k, n_hid)
         return pltpu.make_async_remote_copy(
-            src_ref=blk.at[c], dst_ref=st1.at[c, h], send_sem=d1_s.at[c, to], recv_sem=d1_r.at[c, h],
+            src_ref=blk.at[c], dst_ref=st1.at[c, h], send_sem=d1_s.at[c], recv_sem=d1_r.at[c],
             device_id=(e, to), device_id_type=MESH)
 
-    def spread_in(c, k):
-        src = lax.rem(h + k, n_hid)
-        return pltpu.make_async_remote_copy(
-            src_ref=blk.at[c], dst_ref=st1.at[c, src], send_sem=d1_s.at[c, src], recv_sem=d1_r.at[c, src],
-            device_id=(e, src), device_id_type=MESH)
+    def peers(ref, sem):
+        whole = ref.at[pl.ds(0, n_hid - 1)]
+        return pltpu.make_async_copy(whole, whole, sem)
 
     def to_side(c):
         return pltpu.make_async_remote_copy(
@@ -121,46 +119,70 @@
         lax.fori_loop(1, n_hid, body, 0)
         st1[c, h] = blk[c]
     for c in range(parts):
-        def body(k, carry, c=c):
-            spread_in(c, k).wait_recv()
-            return carry
-        lax.fori_loop(1, n_hid, body, 0)
+        peers(st1.at[c], d1_r.at[c]).wait()
         for k in range(n_hid):
             rl[k * T:(k + 1) * T, :] = st1[c, k].astype(F32)
         xg[c, e] = rl[...].astype(BF16)
         to_side(c).start()
         to_core(c, 0).start()
-    for c in range(parts):
+
+    def forward(c):
         from_side(c).wait_recv()
         to_core(c, 1).start()
-    for c in range(parts):
+
+    def collect(c):
         from_core(c, 0).wait_recv()
         from_core(c, 1).wait_recv()
+        xs[:, c * Nc:(c + 1) * Nc] = xg[c, :, :, 0:Nc].reshape(n_exp * rows, Nc)
+
+    def finish(i, slot, both):
+        g = both[:, 0:FC]
+        hid[:, pl.ds(pl.multiple_of(i * FC, FC), FC)] = (g / (1.0 + jnp.exp(-g)) * both[:, FC:]).astype(BF16)
+
+        @pl.when(i + NS < nF)
+        def _():
+            gate_copy(i + NS, slot).start()
+            up_copy(i + NS, slot).start()
+
+        @pl.when(i == max(nF - NS - 1, 0))
+        def _():
+            for j in range(ahead, J):
+                down_copy(j).start()
+
+    def early(c):
+        def body(i, carry):
+            if c == 0:
+                gate_copy(i, i).wait()
+                up_copy(i, i).wait()
+            both = jnp.dot(xs[:, c * Nc:(c + 1) * Nc], w_gu[i, c * Nc:(c + 1) * Nc, :], preferred_element_type=F32)
+            if c > 0:
+                both = both + part_sum[i]
+            if c < parts - 1:
+                part_sum[i] = both
+            else:
+                finish(i, i, both)
+            return carry
+        return body
+
+    cut = min(2, NS)
+    forward(0)
+    collect(0)
+    for c in range(parts):
+        lax.fori_loop(0, cut, early(c), 0)
+        if c < parts - 1:
+            forward(c + 1)
+        lax.fori_loop(cut, NS, early(c), 0)
+        if c < parts - 1:
+            collect(c + 1)
 
     def ffn(i, carry):
         slot = lax.rem(i, NS)
         gate_copy(i, slot).wait()
         up_copy(i, slot).wait()
-        g = jnp.zeros((n_exp * rows, FC), F32)
-        u = jnp.zeros((n_exp * rows, FC), F32)
-        for c in range(parts):
-            x = xg[c, :, :, 0:Nc].reshape(n_exp * rows, Nc)
-            g = g + jnp.dot(x, w_gate[slot, c * Nc:(c + 1) * Nc, :], preferred_element_type=F32)
-            u = u + jnp.dot(x, w_up[slot, c * Nc:(c + 1) * Nc, :], preferred_element_type=F32)
-        hid[i] = (g / (1.0 + jnp.exp(-g)) * u).astype(BF16)
-
-        @pl.when(i + NS < nF)
-        def _():
-            gate_copy(i + NS, slot).start()
-            up_copy(i + NS, slot).start()
-
-        @pl.when(i == max(nF - NS - 1, 0))
-        def _():
-            for j in range(ahead, J):
-                down_copy(j).start()
+        finish(i, slot, jnp.dot(xs[...], w_gu[slot], preferred_element_type=F32))
         return carry
 
-    lax.fori_loop(0, nF, ffn, 0)
+    lax.fori_loop(NS, nF, ffn, 0)
 
     meta_all = xg[0, :, :, Nc:].reshape(n_exp * rows, LANES).astype(F32)
     lanes = lax.broadcasted_iota(jnp.int32, (n_exp * rows, LANES), 1)
@@ -180,22 +202,14 @@
     def give(j, k):
         to = lax.rem(h + k, n_hid)
         return pltpu.make_async_remote_copy(
-            src_ref=send3.at[j, to], dst_ref=got3.at[j, h], send_sem=c3_s.at[j, to], recv_sem=c3_r.at[j, h],
+            src_ref=send3.at[j, to], dst_ref=got3.at[j, h], send_sem=c3_s.at[j], recv_sem=c3_r.at[j],
             device_id=(e, to), device_id_type=MESH)
-
-    def take(j, k):
-        src = lax.rem(h + k, n_hid)
-        return pltpu.make_async_remote_copy(
-            src_ref=send3.at[j, src], dst_ref=got3.at[j, src], send_sem=c3_s.at[j, src], recv_sem=c3_r.at[j, src],
-            device_id=(e, src), device_id_type=MESH)
 
     def step(i, carry):
         @pl.when(i < J)
         def _():
             down_copy(i).wait()
-            t = jnp.zeros((n_exp * rows, Ncol), F32)
-            for k in range(nF):
-                t = t + jnp.dot(hid[k], w_down[i, k * FC:(k + 1) * FC, :], preferred_element_type=F32)
+            t = jnp.dot(hid[...], w_down[i], preferred_element_type=F32)
             terms[i] = (t * scale).reshape(n_exp, rows, Ncol)
             give_core(i, 1).start()
             give_core(i, 0).start()
@@ -227,17 +241,11 @@
     lax.fori_loop(0, J + 2, step, 0)
 
     for j in range(J):
-        def body(k, carry, j=j):
-            take(j, k).wait_recv()
-            return carry
-        lax.fori_loop(1, n_hid, body, 0)
+        peers(got3.at[j], c3_r.at[j]).wait()
         out_ref[:, j * Ncol:(j + 1) * Ncol] = jnp.sum(got3[j].astype(F32), axis=0).astype(BF16)
 
     for c in range(parts):
-        def body(k, carry, c=c):
-            spread(c, k).wait_send()
-            return carry
-        lax.fori_loop(1, n_hid, body, 0)
+        peers(st1.at[c], d1_s.at[c]).wait()
         to_side(c).wait_send()
         to_core(c, 0).wait_send()
         to_core(c, 1).wait_send()
@@ -246,11 +254,8 @@
         give_core(j, 0).wait_send()
         give_core(j, 1).wait_send()
         give_side(j).wait_send()
-
-        def body(k, c):
-            give(j, k).wait_send()
-            return c
-        return lax.fori_loop(1, n_hid, body, carry)
+        peers(send3.at[j], c3_s.at[j]).wait()
+        return carry
     lax.fori_loop(0, J, sent, 0)
 
 
@@ -265,22 +270,23 @@
     FC = min(256, FFl)
     nF = FFl // FC
     NS = min(5, nF)
-    J = 8
+    J = 6
     Ncol = D // J
-    ahead = min(3, J)
+    ahead = min(2, J)
     rows = n_hid * T
     Nw = Nc + LANES
     cfg = (n_exp, n_hid, T, parts, Nc, FC, nF, NS, J, Ncol, ahead)
     dma = pltpu.SemaphoreType.DMA
     scratch = [
-        pltpu.VMEM((NS, D, FC), BF16),
-        pltpu.VMEM((NS, D, FC), BF16),
+        pltpu.VMEM((NS, D, 2 * FC), BF16),
         pltpu.VMEM((J, FFl, Ncol), BF16),
         pltpu.VMEM((parts, T, Nw), BF16),
         pltpu.VMEM((parts, n_hid, T, Nw), BF16),
         pltpu.VMEM((rows, Nw), F32),
         pltpu.VMEM((parts, n_exp, rows, Nw), BF16),
-        pltpu.VMEM((nF, n_exp * rows, FC), BF16),
+        pltpu.VMEM((n_exp * rows, D), BF16),
+        pltpu.VMEM((NS, n_exp * rows, 2 * FC), F32),
+        pltpu.VMEM((n_exp * rows, FFl), BF16),
         pltpu.VMEM((J, n_exp, rows, Ncol), F32),
         pltpu.VMEM((J, 2, rows, Ncol), F32),
         pltpu.VMEM((J, rows, Ncol), F32),
@@ -290,12 +296,12 @@
         pltpu.VMEM((J, n_hid, T, Ncol), BF16),
         pltpu.VMEM((J, n_hid, T, Ncol), BF16),
         dma((parts,)), dma((NS,)), dma((NS,)), dma((J,)),
-        dma((parts, n_hid)), dma((parts, n_hid)),
+        dma((parts,)), dma((parts,)),
         dma((parts,)), dma((parts,)),
         dma((parts, 2)), dma((parts, 2)),
         dma((J, 2)), dma((J, 2)),
         dma((J,)), dma((J,)),
-        dma((J, n_hid)), dma((J, n_hid)),
+        dma((J,)), dma((J,)),
     ]
     any_spec = pl.BlockSpec(memory_space=pl.ANY)
     vmem = pl.BlockSpec(memory_space=pltpu.VMEM)

time: 65 us -> 61.8 us (0.951)
  Pallas kernels: 63.4 us -> 60.3 us
    pallas_call x1, Pallas kernels: 63.4 us -> 60.3 us  [shards(): pl.pallas_call(functools.partial(kernel, cfg), out_shape=jax.ShapeDtypeSt...]
where the time goes in v2:
time: 61.8 us; the launch traced here: 61.6 us
  Pallas kernels  60.3 us (98%)
  local copies, waits for them, and re-layouts  1.36 us (2%)
    pallas_call x1, Pallas kernels, shards(): pl.pallas_call(functools.partial(kernel, cfg), out_shape=jax.ShapeDtypeSt...  60.3 us
    unnamed x1, local copies, waits for them, and re-layouts  1.36 us

profile of v2, /device:TPU:0, one launch (start us, length us, event | category | flops | bytes accessed | tf_op | source)
XLA Modules:
  0.0 61.6 jit_solution(9932663155564895879)
XLA Ops:
  0.0 60.3 %shard_map.64 = bf16[2,6144]{1,0:T(2,128)(2,1)} custom-call(bf16[2,6144]{1,0:T(2,128)(2,1)} %tok_ref.1, s32[2,2]{1,0:T(2,128)} %routing_ref.1, f32[2,2]{1,0:T(2,128)} %mix_ref.1, bf16[1,6144,2048]{2,1,0:T(8,128)(2,1)} %gate_ref.1, bf16[1,6144,2048]{2,1,0:T(8,128)(2,1)} %up_ref.1, bf16[1,2048,6144]{2,1,0:T(8,128)(2,1)} %down_ref.1), custom_call_target="tpu_custom_call" | custom-call | flops 4831838208 | bytes 75497472 | tf_op jit(solution)/shard_map/pallas_call | solution.py:309
  60.3 1.4 %copy.8 = bf16[2,6144]{1,0:T(2,128)(2,1)} copy(bf16[2,6144]{1,0:T(2,128)(2,1)} %shard_map.64) | data formatting | bytes 49152

commit v3 on v2

--- a/solution.py
+++ b/solution.py
@@ -19,12 +19,13 @@
 
 def kernel(
     cfg, tok_ref, routing_ref, mix_ref, gate_ref, up_ref, down_ref, out_ref,
-    w_gu, w_down, blk, st1, rl, xg, xs, part_sum, hid, terms, got1, acc, send2, got2, rl2, send3, got3,
+    w_gate, w_up, w_down, blk, st1, rl, xg, xs, acc_g, acc_u, hid, terms, got1, acc, send2, got2, rl2, send3, got3,
     sem_tok, sem_gate, sem_up, sem_down,
     d1_s, d1_r, d2_s, d2_r, d3_s, d3_r, c1_s, c1_r, c2_s, c2_r, c3_s, c3_r,
 ):
-    n_exp, n_hid, T, parts, Nc, FC, nF, NS, J, Ncol, ahead = cfg
+    n_exp, n_hid, T, parts, Nc, KC, nK, NB, NS, first, J, Ncol = cfg
     rows = n_hid * T
+    per = nK // parts
     e = lax.axis_index("expert")
     h = lax.axis_index("hidden")
     core = flip(e, 1)
@@ -32,11 +33,11 @@
 
     def gate_copy(i, slot):
         return pltpu.make_async_copy(
-            gate_ref.at[0, :, pl.ds(pl.multiple_of(i * FC, FC), FC)], w_gu.at[slot, :, pl.ds(0, FC)], sem_gate.at[slot])
+            gate_ref.at[0, pl.ds(pl.multiple_of(i * KC, KC), KC)], w_gate.at[slot], sem_gate.at[slot])
 
     def up_copy(i, slot):
         return pltpu.make_async_copy(
-            up_ref.at[0, :, pl.ds(pl.multiple_of(i * FC, FC), FC)], w_gu.at[slot, :, pl.ds(FC, FC)], sem_up.at[slot])
+            up_ref.at[0, pl.ds(pl.multiple_of(i * KC, KC), KC)], w_up.at[slot], sem_up.at[slot])
 
     def down_copy(j):
         return pltpu.make_async_copy(
@@ -48,11 +49,19 @@
 
     for c in range(parts):
         tok_copy(c).start()
-    for i in range(NS):
-        gate_copy(i, i).start()
-        up_copy(i, i).start()
-    for j in range(ahead):
-        down_copy(j).start()
+
+    queue = [("pair", i) for i in range(NS)] + [("down", j) for j in range(J)]
+
+    def fetch(count):
+        for kind, i in queue[:count]:
+            if kind == "pair":
+                gate_copy(i, i).start()
+                up_copy(i, i).start()
+            else:
+                down_copy(i).start()
+        del queue[:count]
+
+    fetch(first)
 
     barrier = pltpu.get_barrier_semaphore()
 
@@ -118,6 +127,7 @@
             return carry
         lax.fori_loop(1, n_hid, body, 0)
         st1[c, h] = blk[c]
+    fetch(2)
     for c in range(parts):
         peers(st1.at[c], d1_r.at[c]).wait()
         for k in range(n_hid):
@@ -125,6 +135,7 @@
         xg[c, e] = rl[...].astype(BF16)
         to_side(c).start()
         to_core(c, 0).start()
+        fetch(1)
 
     def forward(c):
         from_side(c).wait_recv()
@@ -133,56 +144,49 @@
     def collect(c):
         from_core(c, 0).wait_recv()
         from_core(c, 1).wait_recv()
-        xs[:, c * Nc:(c + 1) * Nc] = xg[c, :, :, 0:Nc].reshape(n_exp * rows, Nc)
-
-    def finish(i, slot, both):
-        g = both[:, 0:FC]
-        hid[:, pl.ds(pl.multiple_of(i * FC, FC), FC)] = (g / (1.0 + jnp.exp(-g)) * both[:, FC:]).astype(BF16)
-
-        @pl.when(i + NS < nF)
-        def _():
-            gate_copy(i + NS, slot).start()
-            up_copy(i + NS, slot).start()
-
-        @pl.when(i == max(nF - NS - 1, 0))
-        def _():
-            for j in range(ahead, J):
-                down_copy(j).start()
-
-    def early(c):
-        def body(i, carry):
-            if c == 0:
-                gate_copy(i, i).wait()
-                up_copy(i, i).wait()
-            both = jnp.dot(xs[:, c * Nc:(c + 1) * Nc], w_gu[i, c * Nc:(c + 1) * Nc, :], preferred_element_type=F32)
-            if c > 0:
-                both = both + part_sum[i]
-            if c < parts - 1:
-                part_sum[i] = both
-            else:
-                finish(i, i, both)
-            return carry
-        return body
-
-    cut = min(2, NS)
-    forward(0)
-    collect(0)
-    for c in range(parts):
-        lax.fori_loop(0, cut, early(c), 0)
-        if c < parts - 1:
-            forward(c + 1)
-        lax.fori_loop(cut, NS, early(c), 0)
-        if c < parts - 1:
-            collect(c + 1)
+        for q in range(per):
+            xs[c * per + q] = xg[c, :, :, q * KC:(q + 1) * KC].reshape(n_exp * rows, KC)
+
+    acc_g[...] = jnp.zeros_like(acc_g)
+    acc_u[...] = jnp.zeros_like(acc_u)
 
     def ffn(i, carry):
         slot = lax.rem(i, NS)
         gate_copy(i, slot).wait()
         up_copy(i, slot).wait()
-        finish(i, slot, jnp.dot(xs[...], w_gu[slot], preferred_element_type=F32))
+        x = xs[i]
+        for n in range(0, acc_g.shape[1], NB):
+            acc_g[:, n:n + NB] += jnp.dot(x, w_gate[slot, :, n:n + NB], preferred_element_type=F32)
+            acc_u[:, n:n + NB] += jnp.dot(x, w_up[slot, :, n:n + NB], preferred_element_type=F32)
+
+        @pl.when(i + NS < nK)
+        def _():
+            gate_copy(i + NS, slot).start()
+            up_copy(i + NS, slot).start()
+
+        @pl.when(i == max(nK - NS - 1, 0))
+        def _():
+            for j in left:
+                down_copy(j).start()
         return carry
 
-    lax.fori_loop(NS, nF, ffn, 0)
+    for c in range(parts - 1):
+        forward(c)
+        fetch(1)
+    fetch(max(0, len(queue) - J))
+    left = [j for _, j in queue]
+    collect(0)
+    half = per // 2
+    lax.fori_loop(0, half, ffn, 0)
+    forward(parts - 1)
+    for c in range(parts):
+        if c > 0:
+            collect(c)
+        lo = half if c == 0 else c * per
+        lax.fori_loop(lo, (c + 1) * per, ffn, 0)
+    for n in range(0, acc_g.shape[1], NB):
+        g = acc_g[:, n:n + NB]
+        hid[:, n:n + NB] = (g / (1.0 + jnp.exp(-g)) * acc_u[:, n:n + NB]).astype(BF16)
 
     meta_all = xg[0, :, :, Nc:].reshape(n_exp * rows, LANES).astype(F32)
     lanes = lax.broadcasted_iota(jnp.int32, (n_exp * rows, LANES), 1)
@@ -265,27 +269,30 @@
     n_exp = lax.axis_size("expert")
     n_hid = lax.axis_size("hidden")
     assert n_exp == 4
-    parts = 2
+    parts = 3
     Nc = D // parts
-    FC = min(256, FFl)
-    nF = FFl // FC
-    NS = min(5, nF)
+    KC = 512
+    nK = D // KC
+    NB = min(512, FFl)
+    NS = min(7, nK)
+    first = 3
     J = 6
     Ncol = D // J
-    ahead = min(2, J)
     rows = n_hid * T
     Nw = Nc + LANES
-    cfg = (n_exp, n_hid, T, parts, Nc, FC, nF, NS, J, Ncol, ahead)
+    cfg = (n_exp, n_hid, T, parts, Nc, KC, nK, NB, NS, first, J, Ncol)
     dma = pltpu.SemaphoreType.DMA
     scratch = [
-        pltpu.VMEM((NS, D, 2 * FC), BF16),
+        pltpu.VMEM((NS, KC, FFl), BF16),
+        pltpu.VMEM((NS, KC, FFl), BF16),
         pltpu.VMEM((J, FFl, Ncol), BF16),
         pltpu.VMEM((parts, T, Nw), BF16),
         pltpu.VMEM((parts, n_hid, T, Nw), BF16),
         pltpu.VMEM((rows, Nw), F32),
         pltpu.VMEM((parts, n_exp, rows, Nw), BF16),
-        pltpu.VMEM((n_exp * rows, D), BF16),
-        pltpu.VMEM((NS, n_exp * rows, 2 * FC), F32),
+        pltpu.VMEM((nK, n_exp * rows, KC), BF16),
+        pltpu.VMEM((n_exp * rows, FFl), F32),
+        pltpu.VMEM((n_exp * rows, FFl), F32),
         pltpu.VMEM((n_exp * rows, FFl), BF16),
         pltpu.VMEM((J, n_exp, rows, Ncol), F32),
         pltpu.VMEM((J, 2, rows, Ncol), F32),

time: 61.8 us -> 50.3 us (0.81)
  Pallas kernels: 60.3 us -> 48.8 us
    pallas_call x1, Pallas kernels: 60.3 us -> 48.8 us  [shards(): pl.pallas_call(functools.partial(kernel, cfg), out_shape=jax.ShapeDtypeSt...]
where the time goes in v3:
time: 50.3 us; the launch traced here: 50.1 us
  Pallas kernels  48.8 us (97%)
  local copies, waits for them, and re-layouts  1.36 us (3%)
    pallas_call x1, Pallas kernels, shards(): pl.pallas_call(functools.partial(kernel, cfg), out_shape=jax.ShapeDtypeSt...  48.8 us
    unnamed x1, local copies, waits for them, and re-layouts  1.36 us

profile of v3, /device:TPU:0, one launch (start us, length us, event | category | flops | bytes accessed | tf_op | source)
XLA Modules:
  0.0 50.1 jit_solution(16486609683858991929)
XLA Ops:
  0.0 48.8 %shard_map.64 = bf16[2,6144]{1,0:T(2,128)(2,1)} custom-call(bf16[2,6144]{1,0:T(2,128)(2,1)} %tok_ref.1, s32[2,2]{1,0:T(2,128)} %routing_ref.1, f32[2,2]{1,0:T(2,128)} %mix_ref.1, bf16[1,6144,2048]{2,1,0:T(8,128)(2,1)} %gate_ref.1, bf16[1,6144,2048]{2,1,0:T(8,128)(2,1)} %up_ref.1, bf16[1,2048,6144]{2,1,0:T(8,128)(2,1)} %down_ref.1), custom_call_target="tpu_custom_call" | custom-call | flops 4831838208 | bytes 75497472 | tf_op jit(solution)/shard_map/pallas_call | solution.py:316
  48.8 1.4 %copy.8 = bf16[2,6144]{1,0:T(2,128)(2,1)} copy(bf16[2,6144]{1,0:T(2,128)(2,1)} %shard_map.64) | data formatting | bytes 49152

commit v4 on v3

--- a/solution.py
+++ b/solution.py
@@ -18,9 +18,9 @@
 
 
 def kernel(
-    cfg, tok_ref, routing_ref, mix_ref, gate_ref, up_ref, down_ref, out_ref,
-    w_gate, w_up, w_down, blk, st1, rl, xg, xs, acc_g, acc_u, hid, terms, got1, acc, send2, got2, rl2, send3, got3,
-    sem_tok, sem_gate, sem_up, sem_down,
+    cfg, tok_ref, routing_hbm, mix_hbm, gate_ref, up_ref, down_ref, out_ref,
+    routing_ref, mix_ref, w_gate, w_up, w_down, blk, st1, rl, xg, xs, acc_g, acc_u, hid, terms, got1, acc, send2, got2, rl2, send3, got3,
+    sem_tok, sem_small, sem_gate, sem_up, sem_down,
     d1_s, d1_r, d2_s, d2_r, d3_s, d3_r, c1_s, c1_r, c2_s, c2_r, c3_s, c3_r,
 ):
     n_exp, n_hid, T, parts, Nc, KC, nK, NB, NS, first, J, Ncol = cfg
@@ -47,6 +47,10 @@
         return pltpu.make_async_copy(
             tok_ref.at[:, pl.ds(c * Nc, Nc)], blk.at[c, :, pl.ds(0, Nc)], sem_tok.at[c])
 
+    small = [pltpu.make_async_copy(routing_hbm, routing_ref, sem_small.at[0]),
+             pltpu.make_async_copy(mix_hbm, mix_ref, sem_small.at[1])]
+    for copy in small:
+        copy.start()
     for c in range(parts):
         tok_copy(c).start()
 
@@ -55,10 +59,10 @@
     def fetch(count):
         for kind, i in queue[:count]:
             if kind == "pair":
-                gate_copy(i, i).start()
-                up_copy(i, i).start()
+                gate_copy(i, i).start(priority=1)
+                up_copy(i, i).start(priority=1)
             else:
-                down_copy(i).start()
+                down_copy(i).start(priority=1)
         del queue[:count]
 
     fetch(first)
@@ -73,6 +77,8 @@
     pl.semaphore_signal(barrier, inc=1, device_id=(core, h), device_id_type=MESH)
     pl.semaphore_signal(barrier, inc=1, device_id=(side, h), device_id_type=MESH)
 
+    for copy in small:
+        copy.wait()
     lane = lax.broadcasted_iota(jnp.int32, (T, LANES), 1)
     named = lax.rem(lane, n_exp)
     weight = jnp.zeros((T, LANES), F32)
@@ -161,13 +167,13 @@
 
         @pl.when(i + NS < nK)
         def _():
-            gate_copy(i + NS, slot).start()
-            up_copy(i + NS, slot).start()
+            gate_copy(i + NS, slot).start(priority=1)
+            up_copy(i + NS, slot).start(priority=1)
 
         @pl.when(i == max(nK - NS - 1, 0))
         def _():
             for j in left:
-                down_copy(j).start()
+                down_copy(j).start(priority=1)
         return carry
 
     for c in range(parts - 1):
@@ -246,7 +252,7 @@
 
     for j in range(J):
         peers(got3.at[j], c3_r.at[j]).wait()
-        out_ref[:, j * Ncol:(j + 1) * Ncol] = jnp.sum(got3[j].astype(F32), axis=0).astype(BF16)
+        out_ref[:, j * Ncol:(j + 1) * Ncol] = jnp.sum(got3[j].astype(F32), axis=0)
 
     for c in range(parts):
         peers(st1.at[c], d1_s.at[c]).wait()
@@ -283,6 +289,8 @@
     cfg = (n_exp, n_hid, T, parts, Nc, KC, nK, NB, NS, first, J, Ncol)
     dma = pltpu.SemaphoreType.DMA
     scratch = [
+        pltpu.VMEM(routing.shape, jnp.int32),
+        pltpu.VMEM(mix_weights.shape, F32),
         pltpu.VMEM((NS, KC, FFl), BF16),
         pltpu.VMEM((NS, KC, FFl), BF16),
         pltpu.VMEM((J, FFl, Ncol), BF16),
@@ -302,7 +310,7 @@
         pltpu.VMEM((rows, Ncol), F32),
         pltpu.VMEM((J, n_hid, T, Ncol), BF16),
         pltpu.VMEM((J, n_hid, T, Ncol), BF16),
-        dma((parts,)), dma((NS,)), dma((NS,)), dma((J,)),
+        dma((parts,)), dma((2,)), dma((NS,)), dma((NS,)), dma((J,)),
         dma((parts,)), dma((parts,)),
         dma((parts,)), dma((parts,)),
         dma((parts, 2)), dma((parts, 2)),
@@ -315,14 +323,14 @@
     flops = 6 * n_exp * rows * D * FFl
     return pl.pallas_call(
         functools.partial(kernel, cfg),
-        out_shape=jax.ShapeDtypeStruct((T, D), BF16),
-        in_specs=[any_spec, vmem, vmem, any_spec, any_spec, any_spec],
+        out_shape=jax.ShapeDtypeStruct((T, D), F32),
+        in_specs=[any_spec] * 6,
         out_specs=vmem,
         scratch_shapes=scratch,
         cost_estimate=pl.CostEstimate(flops=flops, bytes_accessed=6 * D * FFl, transcendentals=0),
         compiler_params=pltpu.CompilerParams(
             collective_id=0, has_side_effects=True, vmem_limit_bytes=63 * 1024 * 1024),
-    )(tokens, routing, mix_weights, gate_weight, up_weight, down_weight)
+    )(tokens, routing, mix_weights, gate_weight, up_weight, down_weight).astype(BF16)
 
 
 def solution(mesh):

time: 50.3 us -> 49.7 us (0.988)
  other arithmetic: 0 us -> 1.42 us
  local copies, waits for them, and re-layouts: 1.36 us -> 0 us
  Pallas kernels: 48.8 us -> 48.1 us
    convert_element_type x0 -> x1, other arithmetic: none -> 1.42 us  [shards(): return pl.pallas_call(functools.partial(kernel, cfg), out_shape=jax.Shape...]
    unnamed x1 -> x0, local copies, waits for them, and re-layouts: 1.36 us -> none
    pallas_call x1, Pallas kernels: 48.8 us -> 48.1 us  [shards(): pl.pallas_call(functools.partial(kernel, cfg), out_shape=jax.ShapeDtypeSt...]
where the time goes in v4:
time: 49.7 us; the launch traced here: 49.6 us
  Pallas kernels  48.1 us (97%)
  other arithmetic  1.42 us (3%)
    pallas_call x1, Pallas kernels, shards(): pl.pallas_call(functools.partial(kernel, cfg), out_shape=jax.ShapeDtypeSt...  48.1 us
    convert_element_type x1, other arithmetic, shards(): return pl.pallas_call(functools.partial(kernel, cfg), out_shape=jax.Shape...  1.42 us

profile of v4, /device:TPU:0, one launch (start us, length us, event | category | flops | bytes accessed | tf_op | source)
XLA Modules:
  0.0 49.6 jit_solution(3965492092757968248)
XLA Ops:
  0.0 48.1 %shard_map.64 = f32[2,6144]{1,0:T(2,128)} custom-call(bf16[2,6144]{1,0:T(2,128)(2,1)} %tok_ref.1, s32[2,2]{1,0:T(2,128)} %routing_hbm.1, f32[2,2]{1,0:T(2,128)} %mix_hbm.1, bf16[1,6144,2048]{2,1,0:T(8,128)(2,1)} %gate_ref.1, bf16[1,6144,2048]{2,1,0:T(8,128)(2,1)} %up_ref.1, bf16[1,2048,6144]{2,1,0:T(8,128)(2,1)} %down_ref.1), custom_call_target="tpu_custom_call" | custom-call | flops 4831838208 | bytes 75497472 | tf_op jit(solution)/shard_map/pallas_call | solution.py:324
  48.1 1.4 %convert_element_type.3 = bf16[2,6144]{1,0:T(2,128)(2,1)} convert(f32[2,6144]{1,0:T(2,128)} %shard_map.64) | non-fusion elementwise | flops 12288 | bytes 73728 | tf_op jit(solution)/shard_map/convert_element_type | solution.py:333

commit v5 on v4

--- a/solution.py
+++ b/solution.py
@@ -190,9 +190,10 @@
             collect(c)
         lo = half if c == 0 else c * per
         lax.fori_loop(lo, (c + 1) * per, ffn, 0)
-    for n in range(0, acc_g.shape[1], NB):
-        g = acc_g[:, n:n + NB]
-        hid[:, n:n + NB] = (g / (1.0 + jnp.exp(-g)) * acc_u[:, n:n + NB]).astype(BF16)
+    SB = min(512, acc_g.shape[1])
+    for n in range(0, acc_g.shape[1], SB):
+        g = acc_g[:, n:n + SB]
+        hid[:, n:n + SB] = (g / (1.0 + jnp.exp(-g)) * acc_u[:, n:n + SB]).astype(BF16)
 
     meta_all = xg[0, :, :, Nc:].reshape(n_exp * rows, LANES).astype(F32)
     lanes = lax.broadcasted_iota(jnp.int32, (n_exp * rows, LANES), 1)
@@ -279,7 +280,7 @@
     Nc = D // parts
     KC = 512
     nK = D // KC
-    NB = min(512, FFl)
+    NB = min(1024, FFl)
     NS = min(7, nK)
     first = 3
     J = 6

time: 49.7 us -> 49.7 us (level)
  no operation moved by 1% of the time
where the time goes in v5:
time: 49.7 us; the launch traced here: 49.6 us
  Pallas kernels  48.1 us (97%)
  other arithmetic  1.42 us (3%)
    pallas_call x1, Pallas kernels, shards(): pl.pallas_call(functools.partial(kernel, cfg), out_shape=jax.ShapeDtypeSt...  48.1 us
    convert_element_type x1, other arithmetic, shards(): return pl.pallas_call(functools.partial(kernel, cfg), out_shape=jax.Shape...  1.42 us

profile of v5, /device:TPU:0, one launch (start us, length us, event | category | flops | bytes accessed | tf_op | source)
XLA Modules:
  0.0 49.6 jit_solution(12987117808996510082)
XLA Ops:
  0.0 48.1 %shard_map.64 = f32[2,6144]{1,0:T(2,128)} custom-call(bf16[2,6144]{1,0:T(2,128)(2,1)} %tok_ref.1, s32[2,2]{1,0:T(2,128)} %routing_hbm.1, f32[2,2]{1,0:T(2,128)} %mix_hbm.1, bf16[1,6144,2048]{2,1,0:T(8,128)(2,1)} %gate_ref.1, bf16[1,6144,2048]{2,1,0:T(8,128)(2,1)} %up_ref.1, bf16[1,2048,6144]{2,1,0:T(8,128)(2,1)} %down_ref.1), custom_call_target="tpu_custom_call" | custom-call | flops 4831838208 | bytes 75497472 | tf_op jit(solution)/shard_map/pallas_call | solution.py:325
  48.1 1.4 %convert_element_type.3 = bf16[2,6144]{1,0:T(2,128)(2,1)} convert(f32[2,6144]{1,0:T(2,128)} %shard_map.64) | non-fusion elementwise | flops 12288 | bytes 73728 | tf_op jit(solution)/shard_map/convert_element_type | solution.py:334
